TPU v7x, 512 devices: a whole 4x8x8 slice. The times are simulated.
512 devices in a mesh: rep: 16 (over x, z_hi), feat: 32 (over z_lo, y, core).
Axes of the slice: x: 4, y: 8, z: 8 (z_hi: 4, z_lo: 2; z = z_hi * 2 + z_lo), core: 2. Of those that a mesh axis runs over, the one named last changes fastest.
Arguments:
- basis: float32 [16, 64, 131072], P('rep', None, 'feat'), may hold values from -6 to 6
- stream: bfloat16 [16, 2, 128, 131072], P('rep', None, None, 'feat'), may hold values from -6 to 6
Outputs:
- new_basis: float32 [16, 64, 131072], P('rep', None, 'feat')
All inputs are finite; a program needn't handle non-finite values.
Results may differ from a plain program's by a relative error of at most 0.0003.
Values sent between devices are 32-bit elements; how exact they have to be, the bound alone decides.
No kernel may reach another device: no remote copies, remote signals or barrier semaphores. Data moves between devices by JAX's collectives and lax.ppermute only.
A program may use at most 64 MiB of HBM per device.

v0:
```python
import jax
import jax.numpy as jnp
from jax import lax
from jax.sharding import PartitionSpec as P

FEAT_DEV = 4096
learn_rate = 0.5


def high_dot(left, right):
    return jnp.dot(left, right, precision=lax.Precision.HIGHEST, preferred_element_type=jnp.float32)


def step_sum(partial_value):
    return lax.psum(partial_value, "feat")


def advance(current, proj, rows, step_size):
    cov = high_dot(proj.T, proj)
    drive = high_dot(proj.T, rows)
    shrink = high_dot(cov, current)
    return current + step_size * (drive - shrink)


def per_device(basis, stream):
    start = basis[0]
    batches = stream[0]
    steps_here = batches.shape[0]
    batch_rows = batches.shape[1]
    total_feat = FEAT_DEV * lax.axis_size("feat")
    scale = jnp.sqrt(jnp.float32(total_feat))
    step_size = learn_rate / batch_rows
    current = start
    for step in range(steps_here):
        rows = batches[step]
        proj = step_sum(high_dot(rows, current.T)) / scale
        current = advance(current, proj, rows, step_size)
    replicas = lax.axis_size("rep")
    average = lax.psum(basis, "rep")[0] / replicas
    mixed = current + average - start
    gram = lax.psum(high_dot(mixed, mixed.T), "feat") / total_feat
    lower = jnp.linalg.cholesky(gram)
    result = lax.linalg.triangular_solve(lower, mixed, left_side=True, lower=True)
    return result[None]


def solution(mesh):
    placed = (P("rep", None, "feat"), P("rep", None, None, "feat"))
    return jax.shard_map(
        per_device, mesh=mesh, in_specs=placed, out_specs=P("rep", None, "feat"), check_vma=False
    )
```

profile of v0, /device:TPU:1, one launch (start us, length us, event | category | flops | bytes accessed | tf_op | source)
XLA Modules:
  0.0 365.0 jit_solution(18399803514366530212)
XLA Ops:
  6.5 0.0 all-reduce.2.cloned.1.call-start
  6.5 0.7 all-reduce.2.cloned.1.call-update
  7.3 0.0 copy-start
  7.3 2.8 fusion.11
  10.1 109.9 %psum.28 = f32[128,64]{0,1:T(8,128)S(1)} all-reduce(f32[128,64]{0,1:T(8,128)S(1)} %fusion.11), channel_id=1, replica_groups=mesh['rep'=16,'feat'=32] {'feat'}, use_global_device_ids=true, to_apply=%region_0.0 | all-reduce | flops 8192 | bytes 65536 | tf_op jit(solution)/shard_map/psum | solution.py:15
  120.0 0.2 fusion.25
  120.2 1.8 fusion.9
  122.0 0.0 copy-done
  122.0 0.0 copy-start.1
  122.0 1.1 fusion.3
  123.1 0.5 copy-done.1
  123.6 1.2 convolution_bitcast_fusion.1
  124.8 108.1 %psum.29 = f32[128,64]{0,1:T(8,128)S(1)} all-reduce(f32[128,64]{0,1:T(8,128)S(1)} %convolution_bitcast_fusion.1), channel_id=1, replica_groups=mesh['rep'=16,'feat'=32] {'feat'}, use_global_device_ids=true, to_apply=%region_1.0 | all-reduce | flops 8192 | bytes 65536 | tf_op jit(solution)/shard_map/psum | solution.py:15
  232.9 0.2 fusion.22
  233.1 2.8 fusion.6
  235.8 2.7 fusion.5
  238.6 1.0 fusion.36
  239.6 104.4 %psum.31 = f32[64,64]{0,1:T(8,128)S(1)} all-reduce(f32[64,64]{0,1:T(8,128)S(1)} %fusion.36), channel_id=1, replica_groups=mesh['rep'=16,'feat'=32] {'feat'}, use_global_device_ids=true, to_apply=%region_3.0 | all-reduce | flops 4096 | bytes 32768 | tf_op jit(solution)/shard_map/psum | solution.py:41
  344.0 0.1 copy.4
  344.1 5.8 %cholesky.16 = f32[64,64]{1,0:T(8,128)S(1)} custom-call(f32[64,64]{1,0:T(8,128)S(1)} %fusion.21), custom_call_target="Cholesky" | custom-call | tf_op jit(solution)/shard_map/jit(cholesky)/cholesky | solution.py:42
  350.0 0.6 compare_reduce_fusion
  350.6 0.7 fusion.19
  351.3 4.9 %custom-call.6 = f32[1,64,64]{1,2,0:T(8,128)S(1)} custom-call(f32[1,64,64]{2,1,0:T(8,128)S(1)} %fusion.19), custom_call_target="InvertDiagBlocksLowerTriangular" | custom-call | tf_op jit(solution)/shard_map/triangular_solve | solution.py:43
  356.2 2.0 convolution_bitcast_fusion
  (4 shorter events, 0.0 us)
Async XLA Ops:
  6.5 229.3 %all-reduce.2.cloned.1.call-start = ((), (), s32[]{:S(2)}) async-start(), calls=%async_computation | async-start | bytes 2097152 | tf_op jit(solution)/shard_map/psum | solution.py:39
  7.3 114.8 %copy-start = (f32[1,64,4096]{2,1,0:T(8,128)S(1)}, f32[1,64,4096]{2,1,0:T(8,128)}, u32[]{:S(2)}) copy-start(f32[1,64,4096]{2,1,0:T(8,128)} %param.2) | copy-start | bytes 3145732
  122.0 1.6 copy-start.1
Sparse Core Ops, SparseCore 0:
  10.3 171.0 all-reduce.1
where the time goes:
time: 365 us
  blocking collectives  322 us (88%)
  matrix products  15.7 us (4%)
  between operations  13.5 us (4%)
  other arithmetic  12.1 us (3%)
    psum x2, blocking collectives, step_sum(): return lax.psum(partial_value, 'feat')  218 us
    psum x1, blocking collectives, per_device(): gram = lax.psum(high_dot(mixed, mixed.T), 'feat') / total_feat  104 us
    dot_general x9, matrix products, high_dot(): jnp.dot(left, right, precision=lax.Precision.HIGHEST, preferred_element_t...  13.7 us
  transfers between devices with their start and end apart: 1, of which 0 were waited for; matrix products, arithmetic and copies ran while one was open for 3% of the time, Pallas kernels for 0%

commit v1 on v0

--- a/solution.py
+++ b/solution.py
@@ -5,6 +5,11 @@
 
 FEAT_DEV = 4096
 learn_rate = 0.5
+
+
+def replace_the_modes(t0):
+    later = lax.all_gather(t0, axis_name="feat")
+    return jnp.sum(later, 0)
 
 
 def high_dot(left, right):
@@ -38,7 +43,7 @@
     replicas = lax.axis_size("rep")
     average = lax.psum(basis, "rep")[0] / replicas
     mixed = current + average - start
-    gram = lax.psum(high_dot(mixed, mixed.T), "feat") / total_feat
+    gram = replace_the_modes(high_dot(mixed, mixed.T)) / total_feat
     lower = jnp.linalg.cholesky(gram)
     result = lax.linalg.triangular_solve(lower, mixed, left_side=True, lower=True)
     return result[None]

time: 365 us -> 299 us (0.82)
  blocking collectives: 322 us -> 256 us
    psum x1 -> x0, blocking collectives: 104 us -> none  [per_device(): gram = lax.psum(high_dot(mixed, mixed.T), 'feat') / total_feat]
    all_gather x0 -> x1, blocking collectives: none -> 37.7 us  [replace_the_modes(): later = lax.all_gather(t0, axis_name='feat')]
where the time goes in v1:
time: 299 us; the launch traced here: 298 us
  blocking collectives  256 us (86%)
  matrix products  15.7 us (5%)
  between operations  13.5 us (5%)
  other arithmetic  12.2 us (4%)
    psum x2, blocking collectives, step_sum(): return lax.psum(partial_value, 'feat')  218 us
    all_gather x1, blocking collectives, replace_the_modes(): later = lax.all_gather(t0, axis_name='feat')  37.7 us
    dot_general x9, matrix products, high_dot(): jnp.dot(left, right, precision=lax.Precision.HIGHEST, preferred_element_t...  13.7 us
    another operation x3, other arithmetic, per_device(): lower = jnp.linalg.cholesky(gram)  6.52 us
  transfers between devices with their start and end apart: 1, of which 0 were waited for; matrix products, arithmetic and copies ran while one was open for 3% of the time, Pallas kernels for 0%

profile of v1, /device:TPU:1, one launch (start us, length us, event | category | flops | bytes accessed | tf_op | source)
XLA Modules:
  0.0 298.4 jit_solution(3826956122840111161)
XLA Ops:
  6.5 0.0 all-reduce.2.cloned.1.call-start
  6.5 0.7 all-reduce.2.cloned.1.call-update
  7.3 2.8 fusion.11
  10.1 109.9 %psum.21 = f32[128,64]{0,1:T(8,128)S(1)} all-reduce(f32[128,64]{0,1:T(8,128)S(1)} %fusion.11), channel_id=1, replica_groups=mesh['rep'=16,'feat'=32] {'feat'}, use_global_device_ids=true, to_apply=%region_0.0 | all-reduce | flops 8192 | bytes 65536 | tf_op jit(solution)/shard_map/psum | solution.py:20
  120.0 0.2 fusion.25
  120.2 1.8 fusion.9
  122.0 0.0 copy-done
  122.0 0.0 copy-start.1
  122.0 1.1 fusion.3
  123.1 0.5 copy-done.1
  123.6 1.2 convolution_bitcast_fusion.1
  124.8 108.1 %psum.22 = f32[128,64]{0,1:T(8,128)S(1)} all-reduce(f32[128,64]{0,1:T(8,128)S(1)} %convolution_bitcast_fusion.1), channel_id=1, replica_groups=mesh['rep'=16,'feat'=32] {'feat'}, use_global_device_ids=true, to_apply=%region_1.0 | all-reduce | flops 8192 | bytes 65536 | tf_op jit(solution)/shard_map/psum | solution.py:20
  232.9 0.2 fusion.22
  233.1 2.8 fusion.6
  235.8 2.7 fusion.5
  238.6 1.0 fusion.36
  239.6 37.7 %all-gather = f32[2048,64]{1,0:T(8,128)S(1)} all-gather(f32[64,64]{1,0:T(8,128)S(1)} %fusion.36), channel_id=2, replica_groups=mesh['rep'=16,'feat'=32] {'feat'}, dimensions={0}, use_global_device_ids=true | all-gather | bytes 540672 | tf_op jit(solution)/shard_map/all_gather | solution.py:11
  277.2 0.1 reduce_sum.11
  277.3 0.1 copy.4
  277.4 5.8 %cholesky.16 = f32[64,64]{1,0:T(8,128)S(1)} custom-call(f32[64,64]{1,0:T(8,128)S(1)} %fusion.21), custom_call_target="Cholesky" | custom-call | tf_op jit(solution)/shard_map/jit(cholesky)/cholesky | solution.py:47
  283.3 0.6 compare_reduce_fusion
  283.9 0.7 fusion.19
  284.6 4.9 %custom-call.6 = f32[1,64,64]{1,2,0:T(8,128)S(1)} custom-call(f32[1,64,64]{2,1,0:T(8,128)S(1)} %fusion.19), custom_call_target="InvertDiagBlocksLowerTriangular" | custom-call | tf_op jit(solution)/shard_map/triangular_solve | solution.py:48
  289.5 2.0 convolution_bitcast_fusion
  (4 shorter events, 0.0 us)
Async XLA Ops:
  6.5 229.3 %all-reduce.2.cloned.1.call-start = ((), (), s32[]{:S(2)}) async-start(), calls=%async_computation | async-start | bytes 2097152 | tf_op jit(solution)/shard_map/psum | solution.py:44
  7.3 114.8 %copy-start = (f32[1,64,4096]{2,1,0:T(8,128)S(1)}, f32[1,64,4096]{2,1,0:T(8,128)}, u32[]{:S(2)}) copy-start(f32[1,64,4096]{2,1,0:T(8,128)} %param.2) | copy-start | bytes 3145732
  122.0 1.6 copy-start.1
Sparse Core Ops, SparseCore 0:
  10.3 171.0 all-reduce.1
